TPU v7x, 32 devices: a whole 2x2x4 slice. The times are simulated.
32 devices in a mesh: gx: 8 (over z, y), gy: 4 (over x, core).
Axes of the slice: x: 2, y: 2, z: 4, core: 2. Of those that a mesh axis runs over, the one named last changes fastest.
Arguments:
- flux_perturbation: float32 [2, 4096, 4096], P(None, 'gx', 'gy'), may hold values from -6 to 6
- archived_nominal_heat_levels: float32 [2, 2, 4096, 4096], P(None, None, 'gx', 'gy'), may hold values from -4 to 4
- archived_solidity_labels: int32 [2, 2, 4096, 4096], P(None, None, 'gx', 'gy'), may hold values from 0 to 2
Outputs:
- hess_vec: float32 [2, 4096, 4096], P(None, 'gx', 'gy')
Inputs may be any that keep to these rules, and one draw needn't show every extreme that they name: `archived_solidity_labels`: 0 is solid, 1 mushy, 2 liquid.
All inputs are finite; a program needn't handle non-finite values.
Results may differ from a plain program's by a relative error of at most 0.000061.
Values sent between devices are 32-bit elements; how exact they have to be, the bound alone decides.
A program may use at most 192 MiB of HBM per device.

v0:
```python
import math
import jax
import jax.numpy as jnp
from jax import lax
from jax.sharding import PartitionSpec as P

TIME_STEP = 0.1
OBS_WEIGHT = 10.0
PRIOR_GAIN = 0.005
HIGHEST = lax.Precision.HIGHEST


def with_halo(cells, sides, width):
    for axis, dim in sides:
        count = lax.axis_size(axis)
        ends = count - 1
        head = lax.slice_in_dim(cells, 0, width, axis=dim)
        tail = lax.slice_in_dim(cells, cells.shape[dim] - width, cells.shape[dim], axis=dim)
        cells = jnp.concatenate(
            [
                lax.ppermute(tail, axis, [(i, (i + 1) % count) for i in range(ends)]),
                cells,
                lax.ppermute(head, axis, [((i + 1) % count, i) for i in range(ends)]),
            ],
            axis=dim,
        )
    return cells


def surface_rim(field):
    padded = with_halo(field, (("gx", 1), ("gy", 2)), 1)
    return padded[:, 2:, 1:-1] + padded[:, :-2, 1:-1] + padded[:, 1:-1, 2:] + padded[:, 1:-1, :-2]


def cos_sin(horizontal_line_total, col_count, modulus):
    row_ids = jnp.arange(horizontal_line_total, dtype=jnp.int32)[:, None]
    col_ids = jnp.arange(col_count, dtype=jnp.int32)[None, :]
    angles = (row_ids * col_ids % modulus).astype(jnp.float32) * (2.0 * math.pi / modulus)
    return (jnp.cos(angles), jnp.sin(angles))


def tables(length):
    bit_count = length.bit_length() - 1
    outer_len = 2 ** (bit_count // 2)
    inner_len = length // outer_len
    cos_outer, sin_outer = cos_sin(outer_len, outer_len, outer_len)
    cos_inner, sin_inner = cos_sin(inner_len, inner_len, inner_len)
    twist_cos, twist_sin = cos_sin(outer_len, inner_len, length)
    outer_fwd = jnp.stack([cos_outer, -sin_outer])
    inner_fwd = jnp.stack([jnp.stack([cos_inner, -sin_inner]), jnp.stack([sin_inner, cos_inner])])
    inner_inv = jnp.stack([jnp.stack([cos_inner, sin_inner]), jnp.stack([-sin_inner, cos_inner])])
    outer_inv = jnp.stack([cos_outer, -sin_outer])
    freq_index = (
        jnp.arange(outer_len, dtype=jnp.int32)[:, None]
        + outer_len * jnp.arange(inner_len, dtype=jnp.int32)[None, :]
    )
    signed = jnp.where(freq_index < length // 2, freq_index, freq_index - length).astype(
        jnp.float32
    )
    wave_sq = (signed * (2.0 * math.pi / length)) ** 2
    return (
        length,
        outer_len,
        inner_len,
        outer_fwd,
        inner_fwd,
        inner_inv,
        outer_inv,
        twist_cos,
        twist_sin,
        wave_sq,
    )


def forward(field, table):
    (
        length,
        outer_len,
        inner_len,
        outer_fwd,
        inner_fwd,
        inner_inv,
        outer_inv,
        twist_cos,
        twist_sin,
        wave_sq,
    ) = table
    grid = field.reshape(field.shape[:-1] + (outer_len, inner_len))
    stepped = jnp.einsum("...ab,rak->...rkb", grid, outer_fwd, precision=HIGHEST)
    step_re = stepped[..., 0, :, :]
    step_im = stepped[..., 1, :, :]
    twisted = jnp.stack(
        [step_re * twist_cos + step_im * twist_sin, step_im * twist_cos - step_re * twist_sin],
        axis=-3,
    )
    spec = jnp.einsum("...rkb,rsbm->...skm", twisted, inner_fwd, precision=HIGHEST)
    return (spec[..., 0, :, :], spec[..., 1, :, :])


def inverse(spec_re, spec_im, table):
    (
        length,
        outer_len,
        inner_len,
        outer_fwd,
        inner_fwd,
        inner_inv,
        outer_inv,
        twist_cos,
        twist_sin,
        wave_sq,
    ) = table
    stacked = jnp.stack([spec_re, spec_im], axis=-3)
    halved = jnp.einsum("...skm,srbm->...rkb", stacked, inner_inv, precision=HIGHEST)
    half_re = halved[..., 0, :, :]
    half_im = halved[..., 1, :, :]
    turned = jnp.stack(
        [half_re * twist_cos - half_im * twist_sin, half_im * twist_cos + half_re * twist_sin],
        axis=-3,
    )
    grid = jnp.einsum("...rkb,rka->...ab", turned, outer_inv, precision=HIGHEST)
    return grid.reshape(grid.shape[:-2] + (length,)) / length


def shards(flux_perturbation, archived_nominal_heat_levels, archived_solidity_labels):
    capacity = jnp.where(
        archived_solidity_labels == 0, 1.0, jnp.where(archived_solidity_labels == 1, 4.0, 1.25)
    ).astype(jnp.float32)
    diffusion_advance = jnp.where(
        archived_solidity_labels == 0, 1.0, jnp.where(archived_solidity_labels == 1, 0.6, 0.35)
    ).astype(jnp.float32)
    diffusion_advance = diffusion_advance * (1.0 + 0.5 * jnp.tanh(archived_nominal_heat_levels))
    rows = lax.all_to_all(flux_perturbation, "gx", split_axis=2, concat_axis=1, tiled=True)
    row_table = tables(rows.shape[1])
    first_u = TIME_STEP * flux_perturbation / capacity[0, 0]
    second_top = TIME_STEP * flux_perturbation + TIME_STEP * (
        diffusion_advance[0, 0] * (surface_rim(first_u) - 6.0 * first_u) + flux_perturbation
    )
    second_low = TIME_STEP * diffusion_advance[0, 1] * first_u
    top_u = second_top / capacity[1, 0]
    low_u = second_low / capacity[1, 1]
    third_top = second_top + TIME_STEP * (
        diffusion_advance[1, 0] * (surface_rim(top_u) - 6.0 * top_u + low_u) + flux_perturbation
    )
    misfit = OBS_WEIGHT * third_top / capacity[1, 0]
    adj_three = misfit / capacity[1, 0]
    push_top = TIME_STEP * diffusion_advance[1, 0] * adj_three
    adj_two_top = adj_three + (surface_rim(push_top) - 6.0 * push_top) / capacity[1, 0]
    adj_two_low = push_top / capacity[1, 1]
    pull_top = TIME_STEP * diffusion_advance[0, 0] * adj_two_top
    pull_low = TIME_STEP * diffusion_advance[0, 1] * adj_two_low
    adj_one_top = adj_two_top + (surface_rim(pull_top) - 6.0 * pull_top + pull_low) / capacity[0, 0]
    data_term = TIME_STEP * (adj_three + adj_two_top + adj_one_top)
    row_re, row_im = forward(jnp.swapaxes(rows, 1, 2), row_table)
    wave_x = row_table[-1]
    second_x = jnp.swapaxes(
        inverse(2.0 * PRIOR_GAIN * wave_x * row_re, 2.0 * PRIOR_GAIN * wave_x * row_im, row_table),
        1,
        2,
    )
    fourth_x = jnp.swapaxes(
        inverse(
            PRIOR_GAIN * wave_x * wave_x * row_re, PRIOR_GAIN * wave_x * wave_x * row_im, row_table
        ),
        1,
        2,
    )
    second_back, fourth_part = (
        lax.all_to_all(second_x, "gx", split_axis=1, concat_axis=2, tiled=True),
        lax.all_to_all(fourth_x, "gx", split_axis=1, concat_axis=2, tiled=True),
    )
    cols_dir, cols_second = (
        lax.all_to_all(flux_perturbation, "gy", split_axis=1, concat_axis=2, tiled=True),
        lax.all_to_all(second_back, "gy", split_axis=1, concat_axis=2, tiled=True),
    )
    col_table = tables(cols_dir.shape[2])
    dir_re, dir_im = forward(cols_dir, col_table)
    sec_re, sec_im = forward(cols_second, col_table)
    wave_y = col_table[-1]
    mixed = inverse(
        PRIOR_GAIN * wave_y * wave_y * dir_re + wave_y * sec_re,
        PRIOR_GAIN * wave_y * wave_y * dir_im + wave_y * sec_im,
        col_table,
    )
    mixed_back = lax.all_to_all(mixed, "gy", split_axis=2, concat_axis=1, tiled=True)
    return data_term + fourth_part + mixed_back


def solution(mesh):
    in_specs = (P(None, "gx", "gy"), P(None, None, "gx", "gy"), P(None, None, "gx", "gy"))
    out_specs = P(None, "gx", "gy")
    return jax.shard_map(shards, mesh=mesh, in_specs=in_specs, out_specs=out_specs, check_vma=False)
```

profile of v0, /device:TPU:17, one launch (start us, length us, event | category | flops | bytes accessed | tf_op | source)
XLA Modules:
  0.0 816.4 jit_solution(504303709747888213)
XLA Ops:
  0.0 7.4 copy.232
  12.9 7.2 copy.218
  20.1 40.2 %all-to-all-done.2 = f32[2,512,1024]{2,0,1:T(2,128)} async-done(((f32[2,512,1024]{2,0,1:T(2,128)}), f32[2,512,1024]{2,0,1:T(2,128)}, u32[]{:S(2)}, u32[]{:S(2)}) %all-to-all-start.2) | async-done | bytes 4194336 | tf_op jit(solution)/shard_map/all_to_all | solution.py:173
  60.3 5.8 all-to-all-start
  78.5 13.3 %fusion.81 = f32[2,128,2,64,64]{1,3,4,0,2:T(8,128)} fusion(f32[2,128,64,64]{1,3,2,0:T(8,128)} %bitcast.223, f32[1,64,64]{1,2,0:T(8,128)S(1)} %get-tuple-element.69, f32[1,64,64]{1,2,0:T(8,128)S(1)} %get-tuple-element.70), kind=kOutput, calls=%fused_computation.149 | convolution fusion | flops 1610620928 | bytes 12615680 | tf_op jit(solution)/shard_map/...ab,rak->...rkb/dot_general | solution.py:89
  91.8 63.4 %all-to-all-done = f32[2,512,1024]{1,0,2:T(2,128)} async-done(((f32[2,512,1024]{1,0,2:T(2,128)}), f32[2,512,1024]{1,0,2:T(2,128)}, u32[]{:S(2)}, u32[]{:S(2)}) %all-to-all-start) | async-done | bytes 4194336 | tf_op jit(solution)/shard_map/all_to_all | solution.py:133
  165.6 11.7 %fusion.78 = f32[2,128,2,64,64]{1,3,4,0,2:T(8,128)S(1)} fusion(f32[2,128,64,64]{1,3,2,0:T(8,128)} %bitcast.224, f32[1,64,64]{1,2,0:T(8,128)S(1)} %get-tuple-element.69, f32[1,64,64]{1,2,0:T(8,128)S(1)} %get-tuple-element.70), kind=kOutput, calls=%fused_computation.148 | convolution fusion | flops 1610620928 | bytes 12615680 | tf_op jit(solution)/shard_map/...ab,rak->...rkb/dot_general | solution.py:89
  180.5 12.5 %fusion.87 = f32[2,128,2,64,64]{1,4,3,0,2:T(8,128)S(1)} fusion(f32[2,128,2,64,64]{1,3,4,0,2:T(8,128)S(1)} %pad_maximum_fusion, f32[1,2,64,64]{2,3,1,0:T(8,128)S(1)} %get-tuple-element.61, f32[1,2,64,64]{2,3,1,0:T(8,128)S(1)} %get-tuple-element.64), kind=kOutput, calls=%fused_computation.151 | convolution fusion | flops 3221241856 | bytes 16842752 | tf_op jit(solution)/shard_map/...rkb,rsbm->...skm/dot_general | solution.py:96
  196.6 8.5 %fusion.90 = f32[2,64,2,128,64]{3,1,4,2,0:T(8,128)S(1)} fusion(f32[2,128,1,64,64]{1,4,3,0,2:T(8,128)S(1)} %get-tuple-element.27, f32[2,128,1,64,64]{1,4,3,0,2:T(8,128)S(1)} %get-tuple-element.26, f32[1,2,64,64]{2,3,1,0:T(8,128)S(1)} %get-tuple-element.65, f32[1,2,64,64]{2,3,1,0:T(8,128)S(1)} %get-tuple-element.60), kind=kOutput, calls=%fused_computation.152 | convolution fusion | flops 3223339008 | bytes 16842752 | tf_op jit(solution)/shard_map/...skm,srbm->...rkb/dot_general | solution.py:114
  205.1 8.4 %copy.364 = f32[2,64,2,128,64]{3,4,1,2,0:T(8,128)} copy(f32[2,64,2,128,64]{3,1,4,2,0:T(8,128)S(1)} %fusion.90) | data formatting | bytes 16777216 | tf_op jit(solution)/shard_map/...skm,srbm->...rkb/dot_general | solution.py:114
  213.5 10.7 %fusion.96 = f32[2,64,2,128,64]{3,1,4,2,0:T(8,128)S(1)} fusion(f32[2,128,1,64,64]{1,4,3,0,2:T(8,128)S(1)} %get-tuple-element.38, f32[2,128,1,64,64]{1,4,3,0,2:T(8,128)} %get-tuple-element.39, f32[1,2,64,64]{2,3,1,0:T(8,128)S(1)} %get-tuple-element.65, f32[1,2,64,64]{2,3,1,0:T(8,128)S(1)} %get-tuple-element.60), kind=kOutput, calls=%fused_computation.154 | convolution fusion | flops 3223339008 | bytes 16842752 | tf_op jit(solution)/shard_map/...skm,srbm->...rkb/dot_general | solution.py:114
  224.2 8.5 %copy.363 = f32[2,64,2,128,64]{3,4,1,2,0:T(8,128)} copy(f32[2,64,2,128,64]{3,1,4,2,0:T(8,128)S(1)} %fusion.96) | data formatting | bytes 16777216 | tf_op jit(solution)/shard_map/...skm,srbm->...rkb/dot_general | solution.py:114
  232.7 12.8 %multiply_subtract_fusion.4 = (f32[2,128,1,64,64]{1,3,4,0,2:T(8,128)}, f32[2,128,1,64,64]{1,3,4,0,2:T(8,128)}, f32[2,128,1,64,64]{1,3,4,0,2:T(8,128)}, f32[2,128...) fusion(f32[2,128,2,64,64]{1,3,4,0,2:T(8,128)} %bitcast.221, ...), kind=kLoop, calls=%fused_computation.138 | loop fusion | flops 18874368 | bytes 50364416 | tf_op jit(solution)/shard_map/sub | solution.py:118
  252.9 16.4 %copy.245 = f32[2,4096,128]{2,0,1:T(2,128)} copy(f32[2,4096,128]{2,1,0:T(8,128)S(1)} %bitcast.228) | data formatting | bytes 8388608 | tf_op jit(solution)/shard_map/transpose | solution.py:156
  269.3 8.0 all-to-all-start.3
  282.7 83.3 %all-to-all-done.3 = f32[2,4096,128]{2,0,1:T(2,128)} async-done(((f32[2,4096,128]{2,0,1:T(2,128)}), f32[2,4096,128]{2,0,1:T(2,128)}, u32[]{:S(2)}, u32[]{:S(2)}) %all-to-all-start.3) | async-done | bytes 4194336 | tf_op jit(solution)/shard_map/all_to_all | solution.py:169
  375.9 7.4 copy.248
  383.3 7.3 all-to-all-start.4
  390.5 9.8 %add_multiply_fusion = (f32[2,2,512,1024]{3,2,1,0:T(8,128)}, pred[2,2,512,1024]{3,2,1,0:T(8,128)(4,1)S(1)}, pred[2,2,512,1024]{3,2,1,0:T(8,128)(4,1)S(1)}) fusion(f32[2,2,512,1024]{3,2,1,0:T(8,128)} %param.4, s32[2,2,512,1024]{3,2,1,0:T(8,128)} %param.5), kind=kLoop, calls=%fused_computation.40 | loop fusion | flops 14680064 | bytes 29360128 | tf_op jit(solution)/shard_map/mul | solution.py:132
  423.1 7.3 fusion.67
  432.8 16.2 %copy.229 = f32[2,4096,128]{2,0,1:T(2,128)} copy(f32[2,4096,128]{2,1,0:T(8,128)S(1)} %bitcast.231) | data formatting | bytes 8388608 | tf_op jit(solution)/shard_map/transpose | solution.py:161
  449.0 8.1 all-to-all-start.1
  484.3 14.6 %broadcast_divide_fusion = f32[2,512,1024]{1,2,0:T(8,128)S(1)} fusion(f32[512,1024]{0,1:T(8,128)} %copy.192, f32[2,512,1024]{1,2,0:T(8,128)} %copy.181, f32[2,512,1024]{1,2,0:T(8,128)} %copy-done, f32[2,1,1024]{1,2,0:T(8,128)S(1)} %copy.185, f32[2,1,1024]{1,2,0:T(8,128)} %copy.187, f32[2,514,1]{1,2,0:T(1,128)S(1)} %collective-permute-done.3, ...), kind=kLoop, calls=%fused_computation.166 | loop fusion | flops 19922944 | bytes 16801824 | tf_op jit(solution)/shard_map/div | solution.py:140
  531.5 15.3 %collective-permute-done.4 = f32[2,1,1024]{2,0,1:T(2,128)} collective-permute-done((f32[2,1,1024]{2,0,1:T(2,128)}, f32[2,1,1024]{2,0,1:T(2,128)}, u32[]{:S(2)}, u32[]{:S(2)}) %collective-permute-start.4) | collective-permute-done | bytes 8224 | tf_op jit(solution)/shard_map/ppermute | solution.py:23
  562.7 13.1 %fusion.93 = f32[2,128,2,64,64]{1,4,3,0,2:T(8,128)} fusion(f32[2,128,2,64,64]{1,3,4,0,2:T(8,128)S(1)} %pad_maximum_fusion.2, f32[1,2,64,64]{2,3,1,0:T(8,128)S(1)} %get-tuple-element.61, f32[1,2,64,64]{2,3,1,0:T(8,128)S(1)} %get-tuple-element.64), kind=kOutput, calls=%fused_computation.153 | convolution fusion | flops 3221241856 | bytes 16842752 | tf_op jit(solution)/shard_map/...rkb,rsbm->...skm/dot_general | solution.py:96
  586.6 11.3 %fusion.84 = f32[2,128,2,64,64]{1,3,4,0,2:T(8,128)S(1)} fusion(f32[2,128,64,64]{1,3,2,0:T(8,128)} %bitcast.225, f32[1,64,64]{1,2,0:T(8,128)S(1)} %get-tuple-element.69, f32[1,64,64]{1,2,0:T(8,128)S(1)} %get-tuple-element.70), kind=kOutput, calls=%fused_computation.150 | convolution fusion | flops 1610620928 | bytes 12615680 | tf_op jit(solution)/shard_map/...ab,rak->...rkb/dot_general | solution.py:89
  603.8 15.9 %fusion.99 = f32[2,128,2,64,64]{1,4,3,0,2:T(8,128)S(1)} fusion(f32[2,128,2,64,64]{1,3,4,0,2:T(8,128)} %pad_maximum_fusion.4, f32[1,2,64,64]{2,3,1,0:T(8,128)S(1)} %get-tuple-element.61, f32[1,2,64,64]{2,3,1,0:T(8,128)S(1)} %get-tuple-element.64), kind=kOutput, calls=%fused_computation.155 | convolution fusion | flops 3221241856 | bytes 16842752 | tf_op jit(solution)/shard_map/...rkb,rsbm->...skm/dot_general | solution.py:96
  624.6 10.8 %fusion.102 = f32[2,64,2,128,64]{3,1,4,2,0:T(8,128)S(1)} fusion(f32[2,128,1,64,64]{1,4,3,0,2:T(8,128)} %get-tuple-element.13, f32[2,128,1,64,64]{1,4,3,0,2:T(8,128)} %get-tuple-element.12, f32[1,2,64,64]{2,3,1,0:T(8,128)S(1)} %get-tuple-element.65, f32[1,2,64,64]{2,3,1,0:T(8,128)S(1)} %get-tuple-element.60), kind=kOutput, calls=%fused_computation.156 | convolution fusion | flops 3223339008 | bytes 16842752 | tf_op jit(solution)/shard_map/...skm,srbm->...rkb/dot_general | solution.py:114
  649.5 16.1 %copy.259 = f32[2,128,4096]{1,0,2:T(2,128)} copy(f32[2,128,4096]{1,2,0:T(8,128)S(1)} %bitcast.233) | data formatting | bytes 8388608 | tf_op jit(solution)/shard_map/div | solution.py:122
  670.7 30.2 %broadcast_multiply_fusion.1 = (f32[2,512,1024]{1,2,0:T(8,128)S(1)}, f32[2,512,1024]{1,2,0:T(8,128)}) fusion(f32[512,1024]{0,1:T(8,128)} %copy.203, f32[512,1024]{0,1:T(8,128)} %copy.202, f32[2,512,1024]{1,2,0:T(8,128)} %copy.181, f32[512,1024]{0,1:T(8,128)} %copy.200, f32[512,1024]{0,1:T(8,128)S(1)} %copy.183, f32[512,1024]{0,1:T(8,128)} %copy.199, ...), kind=kLoop, calls=%fused_computation.165 | loop fusion | flops 44040192 | bytes 35700800 | tf_op jit(solution)/shard_map/mul | solution.py:147
  728.9 15.4 %broadcast_multiply_fusion = (f32[2,512,1024]{1,2,0:T(8,128)S(1)}, f32[2,512,1024]{1,2,0:T(8,128)}) fusion(f32[512,1024]{0,1:T(8,128)} %copy.210, f32[2,512,1024]{1,2,0:T(8,128)} %get-tuple-element.8, f32[512,1024]{0,1:T(8,128)} %copy.192, f32[2,512,1024]{1,2,0:T(8,128)} %copy-done.3, f32[2,1,1024]{1,2,0:T(8,128)S(1)} %copy.205, f32[2,1,1024]{1,2,0:T(8,128)} %copy.207, ...), kind=kLoop, calls=%fused_computation.164 | loop fusion | flops 16777216 | bytes 20996128 | tf_op jit(solution)/shard_map/mul | solution.py:150
  791.0 19.8 %fusion.72 = f32[2,512,1024]{1,2,0:T(8,128)} fusion(f32[2,512,1024]{1,2,0:T(8,128)} %copy.262, f32[2,512,8,128]{1,3,2,0:T(8,128)} %copy.231, f32[2,512,1024]{1,2,0:T(8,128)} %get-tuple-element.6, f32[2,512,1024]{1,2,0:T(8,128)} %copy-done.2, f32[2,1,1024]{1,2,0:T(8,128)S(1)} %copy.212, f32[2,1,1024]{1,2,0:T(8,128)} %copy.214, ...), kind=kLoop, calls=%fused_computation.123 | loop fusion | flops 25165824 | bytes 33579040 | tf_op jit(solution)/shard_map/add | solution.py:186
  (141 shorter events, 278.7 us)
Async XLA Ops:
  7.4 52.9 %all-to-all-start.2 = ((f32[2,512,1024]{2,0,1:T(2,128)}), f32[2,512,1024]{2,0,1:T(2,128)}, u32[]{:S(2)}, u32[]{:S(2)}) async-start(f32[2,512,1024]{2,0,1:T(2,128)} %copy.232), calls=%async_computation.2 | async-start | bytes 8388608 | tf_op jit(solution)/shard_map/all_to_all | solution.py:173
  60.3 94.9 %all-to-all-start = ((f32[2,512,1024]{1,0,2:T(2,128)}), f32[2,512,1024]{1,0,2:T(2,128)}, u32[]{:S(2)}, u32[]{:S(2)}) async-start(f32[2,512,1024]{1,0,2:T(2,128)} %copy.218), calls=%async_computation | async-start | bytes 8388608 | tf_op jit(solution)/shard_map/all_to_all | solution.py:133
  67.0 126.1 %copy-start.6 = (f32[64,64]{1,0:T(8,128)}, f32[64,64]{1,0:T(8,128)S(1)}, u32[]{:S(2)}) copy-start(f32[64,64]{1,0:T(8,128)S(1)} %copy.217) | copy-start | bytes 49156
  205.1 27.6 %slice-start.2 = ((s8[8388608]{0:T(1024)(128)(4,1)}), s8[4194304]{0:T(1024)(128)(4,1)S(1)}, s32[]{:S(2)}) async-start(s8[8388608]{0:T(1024)(128)(4,1)} %bitcast.219), calls=%async_computation.8 | async-start | bytes 8388608
  213.5 19.3 %slice-start.3 = ((s8[8388608]{0:T(1024)(128)(4,1)}), s8[4194304]{0:T(1024)(128)(4,1)S(1)}, s32[]{:S(2)}) async-start(s8[8388608]{0:T(1024)(128)(4,1)} %bitcast.219), calls=%async_computation.9 | async-start | bytes 8388608
  269.3 96.7 %all-to-all-start.3 = ((f32[2,4096,128]{2,0,1:T(2,128)}), f32[2,4096,128]{2,0,1:T(2,128)}, u32[]{:S(2)}, u32[]{:S(2)}) async-start(f32[2,4096,128]{2,0,1:T(2,128)} %copy.245), calls=%async_computation.3 | async-start | bytes 8388608 | tf_op jit(solution)/shard_map/all_to_all | solution.py:169
  383.3 65.7 %all-to-all-start.4 = ((f32[2,512,1024]{2,0,1:T(2,128)}), f32[2,512,1024]{2,0,1:T(2,128)}, u32[]{:S(2)}, u32[]{:S(2)}) async-start(f32[2,512,1024]{2,0,1:T(2,128)} %copy.248), calls=%async_computation.4 | async-start | bytes 8388608 | tf_op jit(solution)/shard_map/all_to_all | solution.py:174
  401.9 5.1 copy-start.4
  416.9 46.0 %collective-permute-start = (f32[2,1,1024]{2,0,1:T(2,128)S(1)}, f32[2,1,1024]{2,0,1:T(2,128)S(1)}, u32[]{:S(2)}, u32[]{:S(2)}) collective-permute-start(f32[2,1,1024]{2,0,1:T(2,128)S(1)} %copy.184), channel_id=1, source_target_pairs={{4,0},{8,4},{12,8},{16,12},{20,16},{24,20},{28,24},{5,1},{9,5},{13... | collective-permute-start | bytes 24584 | tf_op jit(solution)/shard_map/ppermute | solution.py:23
  420.9 42.4 %collective-permute-start.1 = (f32[2,1,1024]{2,0,1:T(2,128)}, f32[2,1,1024]{2,0,1:T(2,128)}, u32[]{:S(2)}, u32[]{:S(2)}) collective-permute-start(f32[2,1,1024]{2,0,1:T(2,128)} %copy.186), channel_id=1, source_target_pairs={{0,4},{4,8},{8,12},{12,16},{16,20},{20,24},{24,28},{1,5},{5,9},{9,... | collective-permute-start | bytes 24584 | tf_op jit(solution)/shard_map/ppermute | solution.py:21
  449.0 216.7 %all-to-all-start.1 = ((f32[2,4096,128]{2,0,1:T(2,128)}), f32[2,4096,128]{2,0,1:T(2,128)}, u32[]{:S(2)}, u32[]{:S(2)}) async-start(f32[2,4096,128]{2,0,1:T(2,128)} %copy.229), calls=%async_computation.1 | async-start | bytes 8388608 | tf_op jit(solution)/shard_map/all_to_all | solution.py:170
  466.9 17.4 %collective-permute-start.3 = (f32[2,514,1]{1,2,0:T(1,128)}, f32[2,514,1]{1,2,0:T(1,128)S(1)}, u32[]{:S(2)}, u32[]{:S(2)}) collective-permute-start(f32[2,514,1]{1,2,0:T(1,128)} %get-tuple-element.47), channel_id=1, source_target_pairs={{0,1},{1,2},{2,3},{4,5},{5,6},{6,7},{8,9},{9,10},{10,11},{12,13},{... | collective-permute-start | bytes 12344 | tf_op jit(solution)/shard_map/ppermute | solution.py:21
  471.2 13.0 %collective-permute-start.2 = (f32[2,514,1]{1,2,0:T(1,128)}, f32[2,514,1]{1,2,0:T(1,128)S(1)}, u32[]{:S(2)}, u32[]{:S(2)}) collective-permute-start(f32[2,514,1]{1,2,0:T(1,128)} %get-tuple-element.46), channel_id=1, source_target_pairs={{1,0},{2,1},{3,2},{5,4},{6,5},{7,6},{9,8},{10,9},{11,10},{13,12},{... | collective-permute-start | bytes 12344 | tf_op jit(solution)/shard_map/ppermute | solution.py:23
  498.9 2.1 copy-start.1
  504.8 42.1 %collective-permute-start.4 = (f32[2,1,1024]{2,0,1:T(2,128)}, f32[2,1,1024]{2,0,1:T(2,128)}, u32[]{:S(2)}, u32[]{:S(2)}) collective-permute-start(f32[2,1,1024]{2,0,1:T(2,128)} %copy.193), channel_id=1, source_target_pairs={{4,0},{8,4},{12,8},{16,12},{20,16},{24,20},{28,24},{5,1},{9,5},{13... | collective-permute-start | bytes 24584 | tf_op jit(solution)/shard_map/ppermute | solution.py:23
  510.0 39.5 %collective-permute-start.5 = (f32[2,1,1024]{2,0,1:T(2,128)}, f32[2,1,1024]{2,0,1:T(2,128)}, u32[]{:S(2)}, u32[]{:S(2)}) collective-permute-start(f32[2,1,1024]{2,0,1:T(2,128)} %copy.195), channel_id=1, source_target_pairs={{0,4},{4,8},{8,12},{12,16},{16,20},{20,24},{24,28},{1,5},{5,9},{9,... | collective-permute-start | bytes 24584 | tf_op jit(solution)/shard_map/ppermute | solution.py:21
  551.6 7.6 copy-start.5
  553.2 117.5 %collective-permute-start.7 = (f32[2,514,1]{1,2,0:T(1,128)}, f32[2,514,1]{1,2,0:T(1,128)}, u32[]{:S(2)}, u32[]{:S(2)}) collective-permute-start(f32[2,514,1]{1,2,0:T(1,128)} %get-tuple-element.45), channel_id=1, source_target_pairs={{0,1},{1,2},{2,3},{4,5},{5,6},{6,7},{8,9},{9,10},{10,11},{12,13},{... | collective-permute-start | bytes 12344 | tf_op jit(solution)/shard_map/ppermute | solution.py:21
  557.3 113.4 %collective-permute-start.6 = (f32[2,514,1]{1,2,0:T(1,128)}, f32[2,514,1]{1,2,0:T(1,128)}, u32[]{:S(2)}, u32[]{:S(2)}) collective-permute-start(f32[2,514,1]{1,2,0:T(1,128)} %get-tuple-element.44), channel_id=1, source_target_pairs={{1,0},{2,1},{3,2},{5,4},{6,5},{7,6},{9,8},{10,9},{11,10},{13,12},{... | collective-permute-start | bytes 12344 | tf_op jit(solution)/shard_map/ppermute | solution.py:23
  599.7 20.1 %slice-start = ((s8[8388608]{0:T(1024)(128)(4,1)}), s8[4194304]{0:T(1024)(128)(4,1)S(1)}, s32[]{:S(2)}) async-start(s8[8388608]{0:T(1024)(128)(4,1)} %bitcast.216), calls=%async_computation.6 | async-start | bytes 8388608
  603.8 16.0 %slice-start.1 = ((s8[8388608]{0:T(1024)(128)(4,1)}), s8[4194304]{0:T(1024)(128)(4,1)S(1)}, s32[]{:S(2)}) async-start(s8[8388608]{0:T(1024)(128)(4,1)} %bitcast.216), calls=%async_computation.7 | async-start | bytes 8388608
  603.8 16.0 %copy-start.7 = (f32[64,64]{1,0:T(8,128)S(1)}, f32[64,64]{1,0:T(8,128)}, u32[]{:S(2)}) copy-start(f32[64,64]{1,0:T(8,128)} %copy-done.6) | copy-start | bytes 49156
  603.8 16.0 %copy-start.8 = (f32[64,64]{1,0:T(8,128)S(1)}, f32[64,64]{1,0:T(8,128)}, u32[]{:S(2)}) copy-start(f32[64,64]{1,0:T(8,128)} %copy.238) | copy-start | bytes 49156
  665.7 110.1 %all-to-all-start.5 = ((f32[2,128,4096]{1,0,2:T(2,128)}), f32[2,128,4096]{1,0,2:T(2,128)}, u32[]{:S(2)}, u32[]{:S(2)}) async-start(f32[2,128,4096]{1,0,2:T(2,128)} %copy.259), calls=%async_computation.5 | async-start | bytes 8388608 | tf_op jit(solution)/shard_map/all_to_all | solution.py:185
  705.9 7.4 collective-permute-start.8
  711.3 5.3 collective-permute-start.9
  718.9 9.9 %collective-permute-start.11 = (f32[2,514,1]{1,2,0:T(1,128)S(1)}, f32[2,514,1]{1,2,0:T(1,128)S(1)}, u32[]{:S(2)}, u32[]{:S(2)}) collective-permute-start(f32[2,514,1]{1,2,0:T(1,128)S(1)} %get-tuple-element.43), channel_id=1, source_target_pairs={{0,1},{1,2},{2,3},{4,5},{5,6},{6,7},{8,9},{9,10},{10,11},{12,13},{... | collective-permute-start | bytes 12344 | tf_op jit(solution)/shard_map/ppermute | solution.py:21
  724.0 4.9 collective-permute-start.10
  749.2 5.6 collective-permute-start.12
  751.5 5.3 collective-permute-start.13
  759.0 31.9 %collective-permute-start.15 = (f32[2,514,1]{1,2,0:T(1,128)S(1)}, f32[2,514,1]{1,2,0:T(1,128)S(1)}, u32[]{:S(2)}, u32[]{:S(2)}) collective-permute-start(f32[2,514,1]{1,2,0:T(1,128)S(1)} %get-tuple-element.41), channel_id=1, source_target_pairs={{0,1},{1,2},{2,3},{4,5},{5,6},{6,7},{8,9},{9,10},{10,11},{12,13},{... | collective-permute-start | bytes 12344 | tf_op jit(solution)/shard_map/ppermute | solution.py:21
  763.7 27.2 %collective-permute-start.14 = (f32[2,514,1]{1,2,0:T(1,128)S(1)}, f32[2,514,1]{1,2,0:T(1,128)S(1)}, u32[]{:S(2)}, u32[]{:S(2)}) collective-permute-start(f32[2,514,1]{1,2,0:T(1,128)S(1)} %get-tuple-element.40), channel_id=1, source_target_pairs={{1,0},{2,1},{3,2},{5,4},{6,5},{7,6},{9,8},{10,9},{11,10},{13,12},{... | collective-permute-start | bytes 12344 | tf_op jit(solution)/shard_map/ppermute | solution.py:23
  (3 other events, 6.0 us)
where the time goes:
time: 823 us; the launch traced here: 816 us
  local copies, waits for them, and re-layouts  244 us (30%)
  waiting for transfers between devices  208 us (25%)
  other arithmetic  150 us (18%)
  matrix products  125 us (15%)
  starting transfers between devices  88.5 us (11%)
    all_to_all x1, waiting for transfers between devices, shards(): lax.all_to_all(second_x, 'gx', split_axis=1, concat_axis=2, tiled=True)  83.3 us
    all_to_all x1, waiting for transfers between devices, shards(): lax.all_to_all(flux_perturbation, 'gx', split_axis=2, concat_axis=1, tile...  63.4 us
    dot_general x3, matrix products, forward(): jnp.einsum('...rkb,rsbm->...skm', twisted, inner_fwd, precision=HIGHEST)  41.5 us
    all_to_all x1, waiting for transfers between devices, shards(): lax.all_to_all(flux_perturbation, 'gy', split_axis=1, concat_axis=2, tile...  40.2 us
    dot_general x3, matrix products, forward(): jnp.einsum('...ab,rak->...rkb', grid, outer_fwd, precision=HIGHEST)  36.2 us
    mul x2, other arithmetic, shards(): push_top = TIME_STEP * diffusion_advance[1, 0] * adj_three  35.4 us
    unnamed x29, local copies, waits for them, and re-layouts  30.3 us
    dot_general x3, matrix products, inverse(): jnp.einsum('...skm,srbm->...rkb', stacked, inner_inv, precision=HIGHEST)  30 us
  transfers between devices with their start and end apart: 22, of which 8 were waited for; matrix products, arithmetic and copies ran while one was open for 42% of the time, Pallas kernels for 0%

commit v1 on v0

--- a/solution.py
+++ b/solution.py
@@ -8,6 +8,28 @@
 OBS_WEIGHT = 10.0
 PRIOR_GAIN = 0.005
 HIGHEST = lax.Precision.HIGHEST
+
+
+def split_up(x, dim, length):
+    before, after = (x.shape[:dim], x.shape[dim + 1 :])
+    return jnp.moveaxis(x.reshape(*before, length, -1, *after), dim, 0)
+
+
+def in_order(pieces, dim):
+    dims = list(pieces.shape[1:])
+    dims[dim] *= pieces.shape[0]
+    return jnp.moveaxis(pieces, 0, dim).reshape(dims)
+
+
+def rotated_exchange(array, axis, split_dim, concat_dim):
+    size, here = (lax.axis_size(axis), lax.axis_index(axis))
+    blocks = split_up(array, split_dim, size)
+    outs = [blocks[here]]
+    for turn in range(1, size):
+        sent = blocks[(here + turn) % size]
+        outs.append(lax.ppermute(sent, axis, [(i, (i + turn) % size) for i in range(size)]))
+    blocks = jnp.stack(outs)[(here - jnp.arange(size)) % size]
+    return in_order(blocks, concat_dim)
 
 
 def with_halo(cells, sides, width):
@@ -170,7 +192,7 @@
         lax.all_to_all(fourth_x, "gx", split_axis=1, concat_axis=2, tiled=True),
     )
     cols_dir, cols_second = (
-        lax.all_to_all(flux_perturbation, "gy", split_axis=1, concat_axis=2, tiled=True),
+        rotated_exchange(flux_perturbation, "gy", 1, 2),
         lax.all_to_all(second_back, "gy", split_axis=1, concat_axis=2, tiled=True),
     )
     col_table = tables(cols_dir.shape[2])

time: 823 us -> 767 us (0.932)
  waiting for transfers between devices: 208 us -> 156 us
    all_to_all x1, waiting for transfers between devices: 63.4 us -> 10.1 us  [shards(): lax.all_to_all(flux_perturbation, 'gx', split_axis=2, concat_axis=1, tile...]
    ppermute x0 -> x3, waiting for transfers between devices: none -> 41.7 us  [rotated_exchange(): lax.ppermute(sent, axis, [(i, (i + turn) % size) for i in range(size)])]
    all_to_all x1 -> x0, waiting for transfers between devices: 40.2 us -> none  [shards(): lax.all_to_all(flux_perturbation, 'gy', split_axis=1, concat_axis=2, tile...]
    all_to_all x2 -> x0, local copies, waits for them, and re-layouts: 10.9 us -> none  [shards(): lax.all_to_all(flux_perturbation, 'gy', split_axis=1, concat_axis=2, tile...]
    unnamed x29 -> x30, local copies, waits for them, and re-layouts: 30.3 us -> 22.7 us
  transfers between devices with their start and end apart: 22 -> 24, of which waited for: 8 -> 9; matrix products, arithmetic and copies ran while one was open for 42% -> 45% of each run, Pallas kernels for 0% -> 0%
where the time goes in v1:
time: 767 us; the launch traced here: 762 us
  local copies, waits for them, and re-layouts  241 us (31%)
  waiting for transfers between devices  156 us (20%)
  other arithmetic  154 us (20%)
  matrix products  124 us (16%)
  starting transfers between devices  85.8 us (11%)
    all_to_all x1, waiting for transfers between devices, shards(): lax.all_to_all(second_x, 'gx', split_axis=1, concat_axis=2, tiled=True)  83.3 us
    ppermute x3, waiting for transfers between devices, rotated_exchange(): lax.ppermute(sent, axis, [(i, (i + turn) % size) for i in range(size)])  41.7 us
    dot_general x3, matrix products, forward(): jnp.einsum('...rkb,rsbm->...skm', twisted, inner_fwd, precision=HIGHEST)  41.5 us
    dot_general x3, matrix products, forward(): jnp.einsum('...ab,rak->...rkb', grid, outer_fwd, precision=HIGHEST)  35.8 us
    mul x2, other arithmetic, shards(): push_top = TIME_STEP * diffusion_advance[1, 0] * adj_three  35.1 us
    dot_general x3, matrix products, inverse(): jnp.einsum('...skm,srbm->...rkb', stacked, inner_inv, precision=HIGHEST)  30 us
    ppermute x8, starting transfers between devices, with_halo(): lax.ppermute(tail, axis, [(i, (i + 1) % count) for i in range(ends)])  27.8 us
    div x4, local copies, waits for them, and re-layouts, inverse(): return grid.reshape(grid.shape[:-2] + (length,)) / length  23.4 us
  transfers between devices with their start and end apart: 24, of which 9 were waited for; matrix products, arithmetic and copies ran while one was open for 45% of the time, Pallas kernels for 0%

profile of v1, /device:TPU:17, one launch (start us, length us, event | category | flops | bytes accessed | tf_op | source)
XLA Modules:
  0.0 761.9 jit_solution(11837211286729087269)
XLA Ops:
  0.0 7.2 copy.224
  22.1 20.9 %collective-permute-done.18 = f32[2,128,1024]{2,1,0:T(8,128)} collective-permute-done((f32[2,128,1024]{2,1,0:T(8,128)}, f32[2,128,1024]{2,1,0:T(8,128)}, u32[]{:S(2)}, u32[]{:S(2)}) %collective-permute-start.18) | collective-permute-done | bytes 1048608 | tf_op jit(solution)/shard_map/ppermute | solution.py:30
  43.0 20.8 %collective-permute-done.16 = f32[2,128,1024]{2,1,0:T(8,128)} collective-permute-done((f32[2,128,1024]{2,1,0:T(8,128)S(1)}, f32[2,128,1024]{2,1,0:T(8,128)}, u32[]{:S(2)}, u32[]{:S(2)}) %collective-permute-start.16) | collective-permute-done | bytes 1048608 | tf_op jit(solution)/shard_map/ppermute | solution.py:30
  78.7 13.3 %fusion.81 = f32[2,128,2,64,64]{1,3,4,0,2:T(8,128)} fusion(f32[2,128,64,64]{1,3,2,0:T(8,128)} %bitcast.244, f32[1,64,64]{1,2,0:T(8,128)S(1)} %get-tuple-element.73, f32[1,64,64]{1,2,0:T(8,128)S(1)} %get-tuple-element.74), kind=kOutput, calls=%fused_computation.151 | convolution fusion | flops 1610620928 | bytes 12615680 | tf_op jit(solution)/shard_map/...ab,rak->...rkb/dot_general | solution.py:111
  92.0 10.1 %all-to-all-done = f32[2,512,1024]{1,0,2:T(2,128)} async-done(((f32[2,512,1024]{1,0,2:T(2,128)}), f32[2,512,1024]{1,0,2:T(2,128)}, u32[]{:S(2)}, u32[]{:S(2)}) %all-to-all-start) | async-done | bytes 4194336 | tf_op jit(solution)/shard_map/all_to_all | solution.py:155
  112.5 11.3 %fusion.78 = f32[2,128,2,64,64]{1,3,4,0,2:T(8,128)S(1)} fusion(f32[2,128,64,64]{1,3,2,0:T(8,128)} %bitcast.245, f32[1,64,64]{1,2,0:T(8,128)S(1)} %get-tuple-element.73, f32[1,64,64]{1,2,0:T(8,128)S(1)} %get-tuple-element.74), kind=kOutput, calls=%fused_computation.150 | convolution fusion | flops 1610620928 | bytes 12615680 | tf_op jit(solution)/shard_map/...ab,rak->...rkb/dot_general | solution.py:111
  127.5 12.5 %fusion.87 = f32[2,128,2,64,64]{1,4,3,0,2:T(8,128)S(1)} fusion(f32[2,128,2,64,64]{1,3,4,0,2:T(8,128)S(1)} %pad_maximum_fusion, f32[1,2,64,64]{2,3,1,0:T(8,128)S(1)} %get-tuple-element.65, f32[1,2,64,64]{2,3,1,0:T(8,128)S(1)} %get-tuple-element.68), kind=kOutput, calls=%fused_computation.153 | convolution fusion | flops 3221241856 | bytes 16842752 | tf_op jit(solution)/shard_map/...rkb,rsbm->...skm/dot_general | solution.py:118
  143.5 8.5 %fusion.90 = f32[2,64,2,128,64]{3,1,4,2,0:T(8,128)S(1)} fusion(f32[2,128,1,64,64]{1,4,3,0,2:T(8,128)S(1)} %get-tuple-element.27, f32[2,128,1,64,64]{1,4,3,0,2:T(8,128)S(1)} %get-tuple-element.26, f32[1,2,64,64]{2,3,1,0:T(8,128)S(1)} %get-tuple-element.69, f32[1,2,64,64]{2,3,1,0:T(8,128)S(1)} %get-tuple-element.64), kind=kOutput, calls=%fused_computation.154 | convolution fusion | flops 3223339008 | bytes 16842752 | tf_op jit(solution)/shard_map/...skm,srbm->...rkb/dot_general | solution.py:136
  152.1 8.4 %copy.376 = f32[2,64,2,128,64]{3,4,1,2,0:T(8,128)} copy(f32[2,64,2,128,64]{3,1,4,2,0:T(8,128)S(1)} %fusion.90) | data formatting | bytes 16777216 | tf_op jit(solution)/shard_map/...skm,srbm->...rkb/dot_general | solution.py:136
  160.5 10.7 %fusion.96 = f32[2,64,2,128,64]{3,1,4,2,0:T(8,128)S(1)} fusion(f32[2,128,1,64,64]{1,4,3,0,2:T(8,128)S(1)} %get-tuple-element.38, f32[2,128,1,64,64]{1,4,3,0,2:T(8,128)} %get-tuple-element.39, f32[1,2,64,64]{2,3,1,0:T(8,128)S(1)} %get-tuple-element.69, f32[1,2,64,64]{2,3,1,0:T(8,128)S(1)} %get-tuple-element.64), kind=kOutput, calls=%fused_computation.156 | convolution fusion | flops 3223339008 | bytes 16842752 | tf_op jit(solution)/shard_map/...skm,srbm->...rkb/dot_general | solution.py:136
  171.2 8.5 %copy.375 = f32[2,64,2,128,64]{3,4,1,2,0:T(8,128)} copy(f32[2,64,2,128,64]{3,1,4,2,0:T(8,128)S(1)} %fusion.96) | data formatting | bytes 16777216 | tf_op jit(solution)/shard_map/...skm,srbm->...rkb/dot_general | solution.py:136
  179.7 12.8 %multiply_subtract_fusion.4 = (f32[2,128,1,64,64]{1,3,4,0,2:T(8,128)}, f32[2,128,1,64,64]{1,3,4,0,2:T(8,128)}, f32[2,128,1,64,64]{1,3,4,0,2:T(8,128)}, f32[2,128...) fusion(f32[2,128,2,64,64]{1,3,4,0,2:T(8,128)} %bitcast.242, ...), kind=kLoop, calls=%fused_computation.140 | loop fusion | flops 18874368 | bytes 50364416 | tf_op jit(solution)/shard_map/sub | solution.py:140
  199.9 16.4 %copy.253 = f32[2,4096,128]{2,0,1:T(2,128)} copy(f32[2,4096,128]{2,1,0:T(8,128)S(1)} %bitcast.249) | data formatting | bytes 8388608 | tf_op jit(solution)/shard_map/transpose | solution.py:178
  216.3 7.8 %all-to-all-start.2 = ((f32[2,4096,128]{2,0,1:T(2,128)}), f32[2,4096,128]{2,0,1:T(2,128)}, u32[]{:S(2)}, u32[]{:S(2)}) async-start(f32[2,4096,128]{2,0,1:T(2,128)} %copy.253), calls=%async_computation.2 | async-start | bytes 8388608 | tf_op jit(solution)/shard_map/all_to_all | solution.py:191
  229.5 83.3 %all-to-all-done.2 = f32[2,4096,128]{2,0,1:T(2,128)} async-done(((f32[2,4096,128]{2,0,1:T(2,128)}), f32[2,4096,128]{2,0,1:T(2,128)}, u32[]{:S(2)}, u32[]{:S(2)}) %all-to-all-start.2) | async-done | bytes 4194336 | tf_op jit(solution)/shard_map/all_to_all | solution.py:191
  322.6 7.4 copy.256
  330.0 7.3 all-to-all-start.3
  337.3 9.8 %add_multiply_fusion = (f32[2,2,512,1024]{3,2,1,0:T(8,128)}, pred[2,2,512,1024]{3,2,1,0:T(8,128)(4,1)S(1)}, pred[2,2,512,1024]{3,2,1,0:T(8,128)(4,1)S(1)}) fusion(f32[2,2,512,1024]{3,2,1,0:T(8,128)} %param.4, s32[2,2,512,1024]{3,2,1,0:T(8,128)} %param.5), kind=kLoop, calls=%fused_computation.41 | loop fusion | flops 14680064 | bytes 29360128 | tf_op jit(solution)/shard_map/mul | solution.py:154
  369.8 7.3 fusion.67
  379.6 16.2 %copy.235 = f32[2,4096,128]{2,0,1:T(2,128)} copy(f32[2,4096,128]{2,1,0:T(8,128)S(1)} %bitcast.252) | data formatting | bytes 8388608 | tf_op jit(solution)/shard_map/transpose | solution.py:183
  395.8 8.1 %all-to-all-start.1 = ((f32[2,4096,128]{2,0,1:T(2,128)}), f32[2,4096,128]{2,0,1:T(2,128)}, u32[]{:S(2)}, u32[]{:S(2)}) async-start(f32[2,4096,128]{2,0,1:T(2,128)} %copy.235), calls=%async_computation.1 | async-start | bytes 8388608 | tf_op jit(solution)/shard_map/all_to_all | solution.py:192
  403.9 6.0 slice_bitcast_fusion.2
  431.2 14.5 %broadcast_divide_fusion = f32[2,512,1024]{1,2,0:T(8,128)S(1)} fusion(f32[512,1024]{0,1:T(8,128)} %copy.198, f32[2,512,1024]{1,2,0:T(8,128)} %copy.187, f32[2,512,1024]{1,2,0:T(8,128)} %copy-done, f32[2,1,1024]{1,2,0:T(8,128)S(1)} %copy.191, f32[2,1,1024]{1,2,0:T(8,128)} %copy.193, f32[2,514,1]{1,2,0:T(1,128)S(1)} %collective-permute-done.3, ...), kind=kLoop, calls=%fused_computation.168 | loop fusion | flops 19922944 | bytes 16801824 | tf_op jit(solution)/shard_map/div | solution.py:162
  478.5 15.2 %collective-permute-done.4 = f32[2,1,1024]{2,0,1:T(2,128)} collective-permute-done((f32[2,1,1024]{2,0,1:T(2,128)}, f32[2,1,1024]{2,0,1:T(2,128)}, u32[]{:S(2)}, u32[]{:S(2)}) %collective-permute-start.4) | collective-permute-done | bytes 8224 | tf_op jit(solution)/shard_map/ppermute | solution.py:45
  509.5 13.1 %fusion.93 = f32[2,128,2,64,64]{1,4,3,0,2:T(8,128)} fusion(f32[2,128,2,64,64]{1,3,4,0,2:T(8,128)S(1)} %pad_maximum_fusion.2, f32[1,2,64,64]{2,3,1,0:T(8,128)S(1)} %get-tuple-element.65, f32[1,2,64,64]{2,3,1,0:T(8,128)S(1)} %get-tuple-element.68), kind=kOutput, calls=%fused_computation.155 | convolution fusion | flops 3221241856 | bytes 16842752 | tf_op jit(solution)/shard_map/...rkb,rsbm->...skm/dot_general | solution.py:118
  533.4 11.3 %fusion.84 = f32[2,128,2,64,64]{1,3,4,0,2:T(8,128)S(1)} fusion(f32[2,128,64,64]{1,3,2,0:T(8,128)} %bitcast.246, f32[1,64,64]{1,2,0:T(8,128)S(1)} %get-tuple-element.73, f32[1,64,64]{1,2,0:T(8,128)S(1)} %get-tuple-element.74), kind=kOutput, calls=%fused_computation.152 | convolution fusion | flops 1610620928 | bytes 12615680 | tf_op jit(solution)/shard_map/...ab,rak->...rkb/dot_general | solution.py:111
  550.6 15.9 %fusion.99 = f32[2,128,2,64,64]{1,4,3,0,2:T(8,128)S(1)} fusion(f32[2,128,2,64,64]{1,3,4,0,2:T(8,128)} %pad_maximum_fusion.4, f32[1,2,64,64]{2,3,1,0:T(8,128)S(1)} %get-tuple-element.65, f32[1,2,64,64]{2,3,1,0:T(8,128)S(1)} %get-tuple-element.68), kind=kOutput, calls=%fused_computation.157 | convolution fusion | flops 3221241856 | bytes 16842752 | tf_op jit(solution)/shard_map/...rkb,rsbm->...skm/dot_general | solution.py:118
  571.4 10.8 %fusion.102 = f32[2,64,2,128,64]{3,1,4,2,0:T(8,128)S(1)} fusion(f32[2,128,1,64,64]{1,4,3,0,2:T(8,128)} %get-tuple-element.13, f32[2,128,1,64,64]{1,4,3,0,2:T(8,128)} %get-tuple-element.12, f32[1,2,64,64]{2,3,1,0:T(8,128)S(1)} %get-tuple-element.69, f32[1,2,64,64]{2,3,1,0:T(8,128)S(1)} %get-tuple-element.64), kind=kOutput, calls=%fused_computation.158 | convolution fusion | flops 3223339008 | bytes 16842752 | tf_op jit(solution)/shard_map/...skm,srbm->...rkb/dot_general | solution.py:136
  596.3 16.1 %copy.267 = f32[2,128,4096]{1,0,2:T(2,128)} copy(f32[2,128,4096]{1,2,0:T(8,128)S(1)} %bitcast.254) | data formatting | bytes 8388608 | tf_op jit(solution)/shard_map/div | solution.py:144
  617.5 29.9 %broadcast_multiply_fusion.1 = (f32[2,512,1024]{1,2,0:T(8,128)S(1)}, f32[2,512,1024]{1,2,0:T(8,128)}) fusion(f32[512,1024]{0,1:T(8,128)} %copy.209, f32[512,1024]{0,1:T(8,128)} %copy.208, f32[2,512,1024]{1,2,0:T(8,128)} %copy.187, f32[512,1024]{0,1:T(8,128)} %copy.206, f32[512,1024]{0,1:T(8,128)S(1)} %copy.189, f32[512,1024]{0,1:T(8,128)} %copy.205, ...), kind=kLoop, calls=%fused_computation.167 | loop fusion | flops 44040192 | bytes 35700800 | tf_op jit(solution)/shard_map/mul | solution.py:169
  675.3 15.0 %broadcast_multiply_fusion = (f32[2,512,1024]{1,2,0:T(8,128)S(1)}, f32[2,512,1024]{1,2,0:T(8,128)}) fusion(f32[512,1024]{0,1:T(8,128)} %copy.216, f32[2,512,1024]{1,2,0:T(8,128)} %get-tuple-element.8, f32[512,1024]{0,1:T(8,128)} %copy.198, f32[2,512,1024]{1,2,0:T(8,128)} %copy-done.3, f32[2,1,1024]{1,2,0:T(8,128)S(1)} %copy.211, f32[2,1,1024]{1,2,0:T(8,128)} %copy.213, ...), kind=kLoop, calls=%fused_computation.166 | loop fusion | flops 16777216 | bytes 20996128 | tf_op jit(solution)/shard_map/mul | solution.py:172
  736.9 19.4 %fusion.72 = f32[2,512,1024]{1,2,0:T(8,128)} fusion(f32[2,512,1024]{1,2,0:T(8,128)} %copy.270, f32[2,512,8,128]{1,3,2,0:T(8,128)} %copy.237, f32[2,512,1024]{1,2,0:T(8,128)} %get-tuple-element.6, f32[2,512,1024]{1,2,0:T(8,128)} %copy-done.2, f32[2,1,1024]{1,2,0:T(8,128)S(1)} %copy.218, f32[2,1,1024]{1,2,0:T(8,128)} %copy.220, ...), kind=kLoop, calls=%fused_computation.125 | loop fusion | flops 25165824 | bytes 33579040 | tf_op jit(solution)/shard_map/add | solution.py:208
  (150 shorter events, 285.3 us)
Async XLA Ops:
  7.2 94.9 %all-to-all-start = ((f32[2,512,1024]{1,0,2:T(2,128)}), f32[2,512,1024]{1,0,2:T(2,128)}, u32[]{:S(2)}, u32[]{:S(2)}) async-start(f32[2,512,1024]{1,0,2:T(2,128)} %copy.224), calls=%async_computation | async-start | bytes 8388608 | tf_op jit(solution)/shard_map/all_to_all | solution.py:155
  16.4 26.7 %collective-permute-start.18 = (f32[2,128,1024]{2,1,0:T(8,128)}, f32[2,128,1024]{2,1,0:T(8,128)}, u32[]{:S(2)}, u32[]{:S(2)}) collective-permute-start(f32[2,128,1024]{2,1,0:T(8,128)} %get-tuple-element.59), channel_id=1, source_target_pairs={{0,3},{1,0},{2,1},{3,2},{4,7},{5,4},{6,5},{7,6},{8,11},{9,8},{10,9... | collective-permute-start | bytes 3145736 | tf_op jit(solution)/shard_map/ppermute | solution.py:30
  17.6 25.4 %collective-permute-start.17 = (f32[2,128,1024]{2,1,0:T(8,128)S(1)}, f32[2,128,1024]{2,1,0:T(8,128)}, u32[]{:S(2)}, u32[]{:S(2)}) collective-permute-start(f32[2,128,1024]{2,1,0:T(8,128)S(1)} %get-tuple-element.57), channel_id=1, source_target_pairs={{0,2},{1,3},{2,0},{3,1},{4,6},{5,7},{6,4},{7,5},{8,10},{9,11},{10,... | collective-permute-start | bytes 3145736 | tf_op jit(solution)/shard_map/ppermute | solution.py:30
  18.8 45.0 %collective-permute-start.16 = (f32[2,128,1024]{2,1,0:T(8,128)S(1)}, f32[2,128,1024]{2,1,0:T(8,128)}, u32[]{:S(2)}, u32[]{:S(2)}) collective-permute-start(f32[2,128,1024]{2,1,0:T(8,128)S(1)} %get-tuple-element.58), channel_id=1, source_target_pairs={{0,1},{1,2},{2,3},{3,0},{4,5},{5,6},{6,7},{7,4},{8,9},{9,10},{10,1... | collective-permute-start | bytes 3145736 | tf_op jit(solution)/shard_map/ppermute | solution.py:30
  127.5 12.6 %copy-start.6 = (f32[64,64]{1,0:T(8,128)S(1)}, f32[64,64]{1,0:T(8,128)}, u32[]{:S(2)}) copy-start(f32[64,64]{1,0:T(8,128)} %copy.223) | copy-start | bytes 49156
  127.5 12.6 %copy-start.8 = (f32[64,64]{1,0:T(8,128)S(1)}, f32[64,64]{1,0:T(8,128)}, u32[]{:S(2)}) copy-start(f32[64,64]{1,0:T(8,128)} %copy.247) | copy-start | bytes 49156
  152.0 27.7 %slice-start.2 = ((s8[8388608]{0:T(1024)(128)(4,1)}), s8[4194304]{0:T(1024)(128)(4,1)S(1)}, s32[]{:S(2)}) async-start(s8[8388608]{0:T(1024)(128)(4,1)} %bitcast.240), calls=%async_computation.7 | async-start | bytes 8388608
  160.5 19.3 %slice-start.3 = ((s8[8388608]{0:T(1024)(128)(4,1)}), s8[4194304]{0:T(1024)(128)(4,1)S(1)}, s32[]{:S(2)}) async-start(s8[8388608]{0:T(1024)(128)(4,1)} %bitcast.240), calls=%async_computation.8 | async-start | bytes 8388608
  216.3 96.4 %all-to-all-start.2 = ((f32[2,4096,128]{2,0,1:T(2,128)}), f32[2,4096,128]{2,0,1:T(2,128)}, u32[]{:S(2)}, u32[]{:S(2)}) async-start(f32[2,4096,128]{2,0,1:T(2,128)} %copy.253), calls=%async_computation.2 | async-start | bytes 8388608 | tf_op jit(solution)/shard_map/all_to_all | solution.py:191
  330.0 65.7 %all-to-all-start.3 = ((f32[2,512,1024]{2,0,1:T(2,128)}), f32[2,512,1024]{2,0,1:T(2,128)}, u32[]{:S(2)}, u32[]{:S(2)}) async-start(f32[2,512,1024]{2,0,1:T(2,128)} %copy.256), calls=%async_computation.3 | async-start | bytes 8388608 | tf_op jit(solution)/shard_map/all_to_all | solution.py:196
  363.6 46.3 %collective-permute-start = (f32[2,1,1024]{2,0,1:T(2,128)S(1)}, f32[2,1,1024]{2,0,1:T(2,128)S(1)}, u32[]{:S(2)}, u32[]{:S(2)}) collective-permute-start(f32[2,1,1024]{2,0,1:T(2,128)S(1)} %copy.190), channel_id=1, source_target_pairs={{4,0},{8,4},{12,8},{16,12},{20,16},{24,20},{28,24},{5,1},{9,5},{13... | collective-permute-start | bytes 24584 | tf_op jit(solution)/shard_map/ppermute | solution.py:45
  367.6 42.6 %collective-permute-start.1 = (f32[2,1,1024]{2,0,1:T(2,128)}, f32[2,1,1024]{2,0,1:T(2,128)}, u32[]{:S(2)}, u32[]{:S(2)}) collective-permute-start(f32[2,1,1024]{2,0,1:T(2,128)} %copy.192), channel_id=1, source_target_pairs={{0,4},{4,8},{8,12},{12,16},{16,20},{20,24},{24,28},{1,5},{5,9},{9,... | collective-permute-start | bytes 24584 | tf_op jit(solution)/shard_map/ppermute | solution.py:43
  395.8 216.7 %all-to-all-start.1 = ((f32[2,4096,128]{2,0,1:T(2,128)}), f32[2,4096,128]{2,0,1:T(2,128)}, u32[]{:S(2)}, u32[]{:S(2)}) async-start(f32[2,4096,128]{2,0,1:T(2,128)} %copy.235), calls=%async_computation.1 | async-start | bytes 8388608 | tf_op jit(solution)/shard_map/all_to_all | solution.py:192
  413.8 17.4 %collective-permute-start.3 = (f32[2,514,1]{1,2,0:T(1,128)}, f32[2,514,1]{1,2,0:T(1,128)S(1)}, u32[]{:S(2)}, u32[]{:S(2)}) collective-permute-start(f32[2,514,1]{1,2,0:T(1,128)} %get-tuple-element.47), channel_id=1, source_target_pairs={{0,1},{1,2},{2,3},{4,5},{5,6},{6,7},{8,9},{9,10},{10,11},{12,13},{... | collective-permute-start | bytes 12344 | tf_op jit(solution)/shard_map/ppermute | solution.py:43
  418.2 13.0 %collective-permute-start.2 = (f32[2,514,1]{1,2,0:T(1,128)}, f32[2,514,1]{1,2,0:T(1,128)S(1)}, u32[]{:S(2)}, u32[]{:S(2)}) collective-permute-start(f32[2,514,1]{1,2,0:T(1,128)} %get-tuple-element.46), channel_id=1, source_target_pairs={{1,0},{2,1},{3,2},{5,4},{6,5},{7,6},{9,8},{10,9},{11,10},{13,12},{... | collective-permute-start | bytes 12344 | tf_op jit(solution)/shard_map/ppermute | solution.py:45
  451.7 42.0 %collective-permute-start.4 = (f32[2,1,1024]{2,0,1:T(2,128)}, f32[2,1,1024]{2,0,1:T(2,128)}, u32[]{:S(2)}, u32[]{:S(2)}) collective-permute-start(f32[2,1,1024]{2,0,1:T(2,128)} %copy.199), channel_id=1, source_target_pairs={{4,0},{8,4},{12,8},{16,12},{20,16},{24,20},{28,24},{5,1},{9,5},{13... | collective-permute-start | bytes 24584 | tf_op jit(solution)/shard_map/ppermute | solution.py:45
  456.9 39.4 %collective-permute-start.5 = (f32[2,1,1024]{2,0,1:T(2,128)}, f32[2,1,1024]{2,0,1:T(2,128)}, u32[]{:S(2)}, u32[]{:S(2)}) collective-permute-start(f32[2,1,1024]{2,0,1:T(2,128)} %copy.201), channel_id=1, source_target_pairs={{0,4},{4,8},{8,12},{12,16},{16,20},{20,24},{24,28},{1,5},{5,9},{9,... | collective-permute-start | bytes 24584 | tf_op jit(solution)/shard_map/ppermute | solution.py:43
  500.0 117.4 %collective-permute-start.7 = (f32[2,514,1]{1,2,0:T(1,128)}, f32[2,514,1]{1,2,0:T(1,128)}, u32[]{:S(2)}, u32[]{:S(2)}) collective-permute-start(f32[2,514,1]{1,2,0:T(1,128)} %get-tuple-element.45), channel_id=1, source_target_pairs={{0,1},{1,2},{2,3},{4,5},{5,6},{6,7},{8,9},{9,10},{10,11},{12,13},{... | collective-permute-start | bytes 12344 | tf_op jit(solution)/shard_map/ppermute | solution.py:43
  504.1 113.4 %collective-permute-start.6 = (f32[2,514,1]{1,2,0:T(1,128)}, f32[2,514,1]{1,2,0:T(1,128)}, u32[]{:S(2)}, u32[]{:S(2)}) collective-permute-start(f32[2,514,1]{1,2,0:T(1,128)} %get-tuple-element.44), channel_id=1, source_target_pairs={{1,0},{2,1},{3,2},{5,4},{6,5},{7,6},{9,8},{10,9},{11,10},{13,12},{... | collective-permute-start | bytes 12344 | tf_op jit(solution)/shard_map/ppermute | solution.py:45
  546.5 20.1 %slice-start = ((s8[8388608]{0:T(1024)(128)(4,1)}), s8[4194304]{0:T(1024)(128)(4,1)S(1)}, s32[]{:S(2)}) async-start(s8[8388608]{0:T(1024)(128)(4,1)} %bitcast.237), calls=%async_computation.5 | async-start | bytes 8388608
  550.6 16.0 %slice-start.1 = ((s8[8388608]{0:T(1024)(128)(4,1)}), s8[4194304]{0:T(1024)(128)(4,1)S(1)}, s32[]{:S(2)}) async-start(s8[8388608]{0:T(1024)(128)(4,1)} %bitcast.237), calls=%async_computation.6 | async-start | bytes 8388608
  550.6 16.0 %copy-start.7 = (f32[64,64]{1,0:T(8,128)S(1)}, f32[64,64]{1,0:T(8,128)}, u32[]{:S(2)}) copy-start(f32[64,64]{1,0:T(8,128)} %copy.223) | copy-start | bytes 49156
  550.6 16.0 %copy-start.9 = (f32[64,64]{1,0:T(8,128)S(1)}, f32[64,64]{1,0:T(8,128)}, u32[]{:S(2)}) copy-start(f32[64,64]{1,0:T(8,128)} %copy.246) | copy-start | bytes 49156
  612.4 109.3 %all-to-all-start.4 = ((f32[2,128,4096]{1,0,2:T(2,128)}), f32[2,128,4096]{1,0,2:T(2,128)}, u32[]{:S(2)}, u32[]{:S(2)}) async-start(f32[2,128,4096]{1,0,2:T(2,128)} %copy.267), calls=%async_computation.4 | async-start | bytes 8388608 | tf_op jit(solution)/shard_map/all_to_all | solution.py:207
  652.3 7.4 collective-permute-start.8
  657.7 5.3 collective-permute-start.9
  665.2 9.9 %collective-permute-start.11 = (f32[2,514,1]{1,2,0:T(1,128)S(1)}, f32[2,514,1]{1,2,0:T(1,128)S(1)}, u32[]{:S(2)}, u32[]{:S(2)}) collective-permute-start(f32[2,514,1]{1,2,0:T(1,128)S(1)} %get-tuple-element.43), channel_id=1, source_target_pairs={{0,1},{1,2},{2,3},{4,5},{5,6},{6,7},{8,9},{9,10},{10,11},{12,13},{... | collective-permute-start | bytes 12344 | tf_op jit(solution)/shard_map/ppermute | solution.py:43
  670.3 4.9 collective-permute-start.10
  695.1 5.6 collective-permute-start.12
  697.4 5.3 collective-permute-start.13
  704.9 32.0 %collective-permute-start.15 = (f32[2,514,1]{1,2,0:T(1,128)S(1)}, f32[2,514,1]{1,2,0:T(1,128)S(1)}, u32[]{:S(2)}, u32[]{:S(2)}) collective-permute-start(f32[2,514,1]{1,2,0:T(1,128)S(1)} %get-tuple-element.41), channel_id=1, source_target_pairs={{0,1},{1,2},{2,3},{4,5},{5,6},{6,7},{8,9},{9,10},{10,11},{12,13},{... | collective-permute-start | bytes 12344 | tf_op jit(solution)/shard_map/ppermute | solution.py:43
  709.6 27.3 %collective-permute-start.14 = (f32[2,514,1]{1,2,0:T(1,128)S(1)}, f32[2,514,1]{1,2,0:T(1,128)S(1)}, u32[]{:S(2)}, u32[]{:S(2)}) collective-permute-start(f32[2,514,1]{1,2,0:T(1,128)S(1)} %get-tuple-element.40), channel_id=1, source_target_pairs={{1,0},{2,1},{3,2},{5,4},{6,5},{7,6},{9,8},{10,9},{11,10},{13,12},{... | collective-permute-start | bytes 12344 | tf_op jit(solution)/shard_map/ppermute | solution.py:45
  (6 other events, 20.7 us)
